TPU v7x, 32 devices: a whole 2x2x4 slice. The times are simulated.
32 devices in a mesh: rep: 8 (over z, x), tp: 4 (over y, core).
Axes of the slice: x: 2, y: 2, z: 4, core: 2. Of those that a mesh axis runs over, the one named last changes fastest.
Arguments:
- tokens: bfloat16 [4096, 2048], P(('rep', 'tp')), may hold values from -6 to 6
- cotangent: bfloat16 [4096, 2048], P(('rep', 'tp')), may hold values from -6 to 6
- gate_blocks: bfloat16 [448, 4, 128, 128], P(('rep', 'tp')), may hold values from -6 to 6
- up_blocks: bfloat16 [448, 4, 128, 128], P(('rep', 'tp')), may hold values from -6 to 6
- down_blocks: bfloat16 [448, 4, 128, 128], P(('rep', 'tp')), may hold values from -6 to 6
- gate_rows: int32 [56, 4], P('tp'), may hold values from 0 to 15, as said below
- up_rows: int32 [56, 4], P('tp'), may hold values from 0 to 15, as said below
- down_columns: int32 [56, 4], P('tp'), may hold values from 0 to 15, as said below
- step_index: int32 [1], replicated, may hold values from 0 to 999
Outputs:
- input_grad: bfloat16 [4096, 2048], P(('rep', 'tp'))
- new_gate: bfloat16 [448, 4, 128, 128], P(('rep', 'tp'))
- new_up: bfloat16 [448, 4, 128, 128], P(('rep', 'tp'))
- new_down: bfloat16 [448, 4, 128, 128], P(('rep', 'tp'))
Inputs may be any that keep to these rules, and one draw needn't show every extreme that they name: `gate_rows`: each row lists 4 different block numbers; all rows together name every block number. `up_rows`: each row lists 4 different block numbers; all rows together name every block number. `down_columns`: each row lists 4 different block numbers; all rows together name every block number.
All inputs are finite; a program needn't handle non-finite values.
Results may differ from a plain program's by a relative error of at most 0.008.
Values may be sent and summed in bfloat16 or wider, within the bound.
A program may use at most 192 MiB of HBM per device.

v0:
```python
from functools import partial

import jax
import jax.numpy as jnp
from jax import lax
from jax.sharding import PartitionSpec as P

learn_rate = 0.5


def shortened(x):

    def short(part):
        return part.astype(jnp.bfloat16) if part.dtype == jnp.float32 else part

    return jax.tree.map(short, x)


def passed_along(value, axis, steps):
    count = lax.axis_size(axis)
    pairs = [(source, (source + steps) % count) for source in range(count)]
    return lax.ppermute(value, axis, pairs)


def send_update(block, distance):
    return jax.tree.map(
        lambda part, own: part.astype(own.dtype),
        passed_along(shortened(block), "rep", distance),
        block,
    )


def along_cycle(block, step_index, sender):
    levels = lax.axis_size("rep").bit_length() - 1
    branches = [partial(sender, distance=2**exponent) for exponent in range(levels)]
    return lax.switch(step_index[0] % levels, branches, block)


def updated_of(weight, grad):
    fresh = (weight.astype(jnp.float32) - learn_rate * grad.astype(jnp.float32)).astype(
        jnp.bfloat16
    )
    return lax.optimization_barrier(fresh)


def mean_of(mine, theirs):
    return ((mine.astype(jnp.float32) + theirs.astype(jnp.float32)) * 0.5).astype(jnp.bfloat16)


def block_onehot(indices, count):
    return (indices[:, :, None] == jnp.arange(count, dtype=jnp.int32)[None, None, :]).astype(
        jnp.float32
    )


def per_device(
    tokens,
    cotangent,
    gate_blocks,
    up_blocks,
    down_blocks,
    gate_rows,
    up_rows,
    down_columns,
    step_index,
):
    all_tokens, all_cotangent = (
        lax.all_gather(tokens, "tp", axis=0, tiled=True),
        lax.all_gather(cotangent, "tp", axis=0, tiled=True),
    )
    row_total, width = all_tokens.shape
    edge = gate_blocks.shape[-1]
    keep_count = gate_blocks.shape[1]
    width_blocks = width // edge
    weight_scale = (keep_count * edge) ** (-0.5)
    token_blocks = all_tokens.reshape(row_total, width_blocks, edge)
    cotangent_blocks = all_cotangent.reshape(row_total, width_blocks, edge)
    gate_input = jnp.take(token_blocks, gate_rows, axis=1)
    up_input = jnp.take(token_blocks, up_rows, axis=1)
    gate = weight_scale * jnp.einsum(
        "rjkc,jkcd->rjd", gate_input, gate_blocks, preferred_element_type=jnp.float32
    )
    up = weight_scale * jnp.einsum(
        "rjkc,jkcd->rjd", up_input, up_blocks, preferred_element_type=jnp.float32
    )
    sigmoid_gate = jax.nn.sigmoid(gate)
    activated = gate * sigmoid_gate
    hidden = (activated * up).astype(jnp.bfloat16)
    down_input = jnp.take(cotangent_blocks, down_columns, axis=1)
    hidden_grad = weight_scale * jnp.einsum(
        "rjkd,jkcd->rjc", down_input, down_blocks, preferred_element_type=jnp.float32
    )
    down_grad = (
        weight_scale
        * jnp.einsum("rjc,rjkd->jkcd", hidden, down_input, preferred_element_type=jnp.float32)
    ).astype(jnp.bfloat16)
    gate_signal = (hidden_grad * up * sigmoid_gate * (1.0 + gate * (1.0 - sigmoid_gate))).astype(
        jnp.bfloat16
    )
    up_signal = (hidden_grad * activated).astype(jnp.bfloat16)
    gate_grad = (
        weight_scale
        * jnp.einsum("rjkc,rjd->jkcd", gate_input, gate_signal, preferred_element_type=jnp.float32)
    ).astype(jnp.bfloat16)
    up_grad = (
        weight_scale
        * jnp.einsum("rjkc,rjd->jkcd", up_input, up_signal, preferred_element_type=jnp.float32)
    ).astype(jnp.bfloat16)
    gate_onehot = block_onehot(gate_rows, width_blocks)
    up_onehot = block_onehot(up_rows, width_blocks)
    own_rows = row_total // lax.axis_size("tp")
    gate_back = jnp.einsum(
        "rjd,jkcd->rjkc", gate_signal, gate_blocks, preferred_element_type=jnp.float32
    )
    up_back = jnp.einsum("rjd,jkcd->rjkc", up_signal, up_blocks, preferred_element_type=jnp.float32)
    total = jnp.einsum("rjkc,jkb->rbc", gate_back, gate_onehot, precision=lax.Precision.HIGHEST)
    total = total + jnp.einsum("rjkc,jkb->rbc", up_back, up_onehot, precision=lax.Precision.HIGHEST)
    input_sum = lax.psum_scatter(
        (weight_scale * total).reshape(own_rows * lax.axis_size("tp"), width),
        "tp",
        scatter_dimension=0,
        tiled=True,
    )
    input_grad = input_sum.astype(jnp.bfloat16)
    own_gate = updated_of(gate_blocks, gate_grad)
    own_up = updated_of(up_blocks, up_grad)
    own_down = updated_of(down_blocks, down_grad)
    received = along_cycle(jnp.stack([own_gate, own_up, own_down]), step_index, send_update)
    peer_gate, peer_up, peer_down = (received[0], received[1], received[2])
    new_gate = mean_of(own_gate, peer_gate)
    new_up = mean_of(own_up, peer_up)
    new_down = mean_of(own_down, peer_down)
    return (input_grad, new_gate, new_up, new_down)


def solution(mesh):
    placed = (
        P(("rep", "tp"), None),
        P(("rep", "tp"), None),
        P(("rep", "tp"), None, None, None),
        P(("rep", "tp"), None, None, None),
        P(("rep", "tp"), None, None, None),
        P("tp", None),
        P("tp", None),
        P("tp", None),
        P(),
    )
    return jax.shard_map(
        per_device,
        mesh=mesh,
        in_specs=placed,
        out_specs=(
            P(("rep", "tp"), None),
            P(("rep", "tp"), None, None, None),
            P(("rep", "tp"), None, None, None),
            P(("rep", "tp"), None, None, None),
        ),
        check_vma=False,
    )
```

profile of v0, /device:TPU:0, one launch (start us, length us, event | category | flops | bytes accessed | tf_op | source)
XLA Modules:
  0.0 440.9 jit_solution(11398162067570812704)
XLA Ops:
  7.2 0.0 all-gather.5.cloned.1.call-start
  7.2 2.0 copy.48
  9.3 0.0 all-gather.3.cloned.1.call-start
  9.3 2.0 copy.42
  11.4 0.0 reduce-scatter.2.cloned.1.call-start
  11.4 0.7 compare_select_fusion.1
  12.1 0.1 copy.49
  12.2 0.1 reshape.72
  12.3 0.7 compare_and_fusion.1
  13.0 0.1 copy.47
  13.1 0.7 compare_select_fusion
  13.8 0.1 copy.54
  13.9 0.1 reshape.76
  14.0 0.7 compare_and_fusion
  14.7 0.1 copy.53
  14.8 0.7 compare_select_fusion.2
  15.5 0.1 copy.43
  15.6 0.1 reshape.68
  15.7 0.7 compare_and_fusion.2
  16.4 0.1 copy.41
  16.5 19.2 %all-gather.5.cloned.1.call-done = bf16[512,2048]{0,1:T(8,128)(2,1)} async-done(((bf16[128,2048]{0,1:T(8,128)(2,1)}), bf16[512,2048]{0,1:T(8,128)(2,1)}) %all-gather.5.cloned.1.call-update) | async-done | bytes 2097168 | tf_op jit(solution)/shard_map/all_gather | solution.py:68
  35.7 3.0 copy.50
  38.7 5.3 %gather_fusion.1 = bf16[56,512,128]{2,1,0:T(8,128)(2,1)} fusion(bf16[512,16,128]{2,0,1:T(8,128)(2,1)S(1)} %copy.50, s32[1024]{0:T(1024)S(1)} %pad_clamp_fusion.1), kind=kCustom, calls=%fused_computation.1.clone | custom fusion | bytes 14680288 | tf_op jit(solution)/shard_map/jit(_take)/gather | solution.py:79
  44.1 10.6 %copy.51 = bf16[14,4,512,128]{2,3,1,0:T(8,128)(2,1)} copy(bf16[14,4,512,128]{3,2,1,0:T(8,128)(2,1)} %bitcast.186) | data formatting | bytes 14680064 | tf_op jit(solution)/shard_map/jit(_take)/gather | solution.py:79
  54.7 5.2 %gather_fusion.2 = bf16[56,512,128]{2,1,0:T(8,128)(2,1)} fusion(bf16[512,16,128]{2,0,1:T(8,128)(2,1)S(1)} %copy.50, s32[1024]{0:T(1024)S(1)} %pad_clamp_fusion), kind=kCustom, calls=%fused_computation.2.clone | custom fusion | bytes 14680288 | tf_op jit(solution)/shard_map/jit(_take)/gather | solution.py:78
  59.9 10.5 %copy.56 = bf16[14,4,512,128]{2,3,1,0:T(8,128)(2,1)} copy(bf16[14,4,512,128]{3,2,1,0:T(8,128)(2,1)} %bitcast.184) | data formatting | bytes 14680064 | tf_op jit(solution)/shard_map/jit(_take)/gather | solution.py:78
  70.5 3.0 copy.44
  73.5 5.2 %gather_fusion = bf16[56,512,128]{2,1,0:T(8,128)(2,1)} fusion(bf16[512,16,128]{2,0,1:T(8,128)(2,1)S(1)} %copy.44, s32[1024]{0:T(1024)S(1)} %pad_clamp_fusion.2), kind=kCustom, calls=%fused_computation.clone | custom fusion | bytes 14680288 | tf_op jit(solution)/shard_map/jit(_take)/gather | solution.py:89
  78.7 10.9 %copy.45 = bf16[14,4,512,128]{2,3,1,0:T(8,128)(2,1)} copy(bf16[14,4,512,128]{3,2,1,0:T(8,128)(2,1)} %bitcast.185) | data formatting | bytes 14680064 | tf_op jit(solution)/shard_map/jit(_take)/gather | solution.py:89
  89.6 8.0 %fusion.10 = f32[14,512,128,1]{2,1,3,0:T(8,128)} fusion(bf16[14,4,128,128]{3,2,1,0:T(8,128)(2,1)} %param.17, bf16[14,4,512,128]{2,3,1,0:T(8,128)(2,1)} %copy.51, pred[14,4]{1,0:T(8,128)(4,1)S(1)} %copy.47), kind=kOutput, calls=%fused_computation.15 | convolution fusion | flops 943194112 | bytes 12845112 | tf_op jit(solution)/shard_map/rjkc,jkcd->rjd/dot_general | solution.py:83
  97.6 4.3 fusion.6
  101.9 9.9 %fusion.28 = (bf16[512,14,128]{2,0,1:T(8,128)(2,1)S(1)}, bf16[512,14,128,1]{2,0,3,1:T(8,128)(2,1)S(1)}) fusion(f32[14,512,128,1]{2,1,3,0:T(8,128)} %fusion.10, f32[14,512,128,1]{2,1,3,0:T(8,128)} %fusion.6, bf16[14,4,128,128]{3,2,1,0:T(8,128)(2,1)} %param.18, bf16[14,4,512,128]{2,3,1,0:T(8,128)(2,1)} %copy.45, pred[14,4]{1,0:T(8,128)(4,1)S(1)} %copy.41), kind=kOutput, calls=%fused_computation.46 | convolution fusion | flops 957874176 | bytes 20185144 | tf_op jit(solution)/shard_map/rjkd,jkcd->rjc/dot_general | solution.py:90
  111.8 2.1 convolution_bitcast_fusion
  114.0 17.2 %fusion = f32[16,512,128,1]{2,0,3,1:T(8,128)S(1)} fusion(f32[512,14,4,128]{3,0,2,1:T(8,128)S(1)} %convolution_bitcast_fusion, s32[14,4]{0,1:T(4,128)S(1)} %copy-done.8), kind=kOutput, calls=%fused_computation.3 | convolution fusion | flops 704643968 | bytes 18874592 | tf_op jit(solution)/shard_map/rjkc,jkb->rbc/dot_general | solution.py:117
  131.2 2.1 convolution_bitcast_fusion.1
  133.2 16.8 %fusion.16 = f32[16,512,128]{2,0,1:T(8,128)S(1)} fusion(f32[16,512,128,1]{2,0,3,1:T(8,128)S(1)} %fusion, f32[512,14,4,128]{3,0,2,1:T(8,128)S(1)} %convolution_bitcast_fusion.1, s32[14,4]{0,1:T(4,128)S(1)} %copy-done.7), kind=kOutput, calls=%fused_computation.27 | convolution fusion | flops 706741120 | bytes 23068896 | tf_op jit(solution)/shard_map/rjkc,jkb->rbc/dot_general | solution.py:116
  150.1 4.2 copy.81
  154.3 4.0 copy.60
  159.0 9.3 %subtract_convert_fusion.1 = bf16[14,4,128,128]{3,2,1,0:T(8,128)(2,1)} fusion(bf16[14,4,128,128]{3,2,1,0:T(8,128)(2,1)} %param.16, bf16[512,14,128]{2,0,1:T(8,128)(2,1)} %copy-done.6, bf16[14,4,512,128]{2,3,1,0:T(8,128)(2,1)} %copy.56, pred[14,4]{1,0:T(8,128)(4,1)S(1)} %copy.53), kind=kOutput, calls=%fused_computation.65 | convolution fusion | flops 949616640 | bytes 12845112 | tf_op jit(solution)/shard_map/rjkc,rjd->jkcd/dot_general | solution.py:103
  168.4 3.4 subtract_convert_fusion
  171.8 8.4 %bitcast_subtract_fusion = bf16[14,4,128,128]{2,3,1,0:T(8,128)(2,1)} fusion(bf16[14,4,128,128]{2,3,1,0:T(8,128)(2,1)} %copy.60, f32[14,512,128,1]{2,1,3,0:T(8,128)} %fusion.10, bf16[14,4,512,128]{2,3,1,0:T(8,128)(2,1)S(1)} %bitcast.195, pred[14,4]{1,0:T(8,128)(4,1)S(1)} %copy.41, f32[14,512,128,1]{2,1,3,0:T(8,128)} %fusion.6), kind=kOutput, calls=%fused_computation.37 | convolution fusion | flops 956956672 | bytes 18350136 | tf_op jit(solution)/shard_map/rjc,rjkd->jkcd/dot_general | solution.py:95
  180.2 2.9 copy.61
  183.1 2.6 pad_maximum_fusion
  185.8 240.0 %conditional.1 = (bf16[3,14,4,128,128]{4,3,2,1,0:T(8,128)(2,1)}) conditional(s32[]{:T(128)} %clamp.3, bf16[3,14,4,128,128]{4,3,2,1,0:T(8,128)(2,1)S(1)} %pad_maximum_fusion, bf16[3,14,4,128,128]{4,3,2,1,0:T(8,128)(2,1)S(1)} %pad_maximum_fusion, bf16[3,14,4,128,128]{4,3,2,1,0:T(8,128)(2,1)S(1)} %pad_maximum_fusion), branch_computations={%region_1.3_spmd, %region_2.4_spmd, %region_3.5_spmd} | conditional | bytes 22020144 | solution.py:36
  185.8 2.6 collective-permute-start.2
  188.4 237.4 %collective-permute-done.2 = bf16[3,14,4,128,128]{4,3,2,1,0:T(8,128)(2,1)} collective-permute-done((bf16[3,14,4,128,128]{4,3,2,1,0:T(8,128)(2,1)S(1)}, bf16[3,14,4,128,128]{4,3,2,1,0:T(8,128)(2,1)}, u32[]{:S(2)}, u32[]{:S(2)}) %collective-permute-start.2) | collective-permute-done | bytes 5505056 | tf_op jit(solution)/shard_map/cond/branch_2_fun/ppermute | solution.py:22
  425.7 6.1 %fusion.18 = (bf16[14,4,128,128]{3,2,1,0:T(8,128)(2,1)}, bf16[14,4,128,128]{3,2,1,0:T(8,128)(2,1)}, bf16[14,4,128,128]{3,2,1,0:T(8,128)(2,1)}) fusion(bf16[14,4,128,128]{3,2,1,0:T(8,128)(2,1)S(1)} %copy.61, bf16[3,14,4,128,128]{4,3,2,1,0:T(8,128)(2,1)} %get-tuple-element.17, bf16[14,4,128,128]{3,2,1,0:T(8,128)(2,1)} %subtract_convert_fusion, ...), kind=kLoop, calls=%fused_computation.30 | loop fusion | flops 13762560 | bytes 16515072 | tf_op jit(solution)/shard_map/convert_element_type | solution.py:47
  431.8 2.1 convert_element_type.90
  (41 shorter events, 0.2 us)
Async XLA Ops:
  7.2 28.5 %all-gather.5.cloned.1.call-start = ((), (), s32[]{:S(2)}) async-start(), calls=%async_computation.2 | async-start | bytes 2621440 | tf_op jit(solution)/shard_map/all_gather | solution.py:68
  9.3 61.2 %all-gather.3.cloned.1.call-start = ((), (), s32[]{:S(2)}) async-start(), calls=%async_computation.1 | async-start | bytes 2621440 | tf_op jit(solution)/shard_map/all_gather | solution.py:69
  11.4 420.5 %reduce-scatter.2.cloned.1.call-start = ((), (), s32[]{:S(2)}) async-start(), calls=%async_computation.3 | async-start | bytes 5242880 | tf_op jit(solution)/shard_map/reduce_scatter | solution.py:118
  78.7 18.9 %slice-start.2 = ((s8[7340032]{0:T(1024)(128)(4,1)}), s8[3145728]{0:T(1024)(128)(4,1)S(1)}, s32[]{:S(2)}) async-start(s8[7340032]{0:T(1024)(128)(4,1)} %bitcast.192), calls=%async_computation.6 | async-start | bytes 6291456
  89.6 8.0 %slice-start.3 = ((s8[7340032]{0:T(1024)(128)(4,1)}), s8[4194304]{0:T(1024)(128)(4,1)S(1)}, s32[]{:S(2)}) async-start(s8[7340032]{0:T(1024)(128)(4,1)} %bitcast.192), calls=%async_computation.7 | async-start | bytes 8388608
  89.6 8.0 %copy-start = (bf16[14,4,128,128]{3,2,1,0:T(8,128)(2,1)S(1)}, bf16[14,4,128,128]{3,2,1,0:T(8,128)(2,1)}, u32[]{:S(2)}) copy-start(bf16[14,4,128,128]{3,2,1,0:T(8,128)(2,1)} %param.16) | copy-start | bytes 5505028
  101.9 9.9 %copy-start.2 = (bf16[14,4,128,128]{3,2,1,0:T(8,128)(2,1)S(1)}, bf16[14,4,128,128]{3,2,1,0:T(8,128)(2,1)}, u32[]{:S(2)}) copy-start(bf16[14,4,128,128]{3,2,1,0:T(8,128)(2,1)} %param.17) | copy-start | bytes 5505028
  111.8 2.1 copy-start.4
  111.8 19.3 %copy-start.6 = (bf16[512,14,128]{2,0,1:T(8,128)(2,1)}, bf16[512,14,128]{2,0,1:T(8,128)(2,1)S(1)}, u32[]{:S(2)}) copy-start(bf16[512,14,128]{2,0,1:T(8,128)(2,1)S(1)} %get-tuple-element.12) | copy-start | bytes 5505028
  111.8 2.1 copy-start.8
  113.9 17.2 %copy-start.1 = (bf16[14,4,128,128]{3,2,1,0:T(8,128)(2,1)S(1)}, bf16[14,4,128,128]{3,2,1,0:T(8,128)(2,1)}, u32[]{:S(2)}) copy-start(bf16[14,4,128,128]{3,2,1,0:T(8,128)(2,1)} %param.16) | copy-start | bytes 5505028
  131.1 2.1 copy-start.7
  154.3 14.0 %slice-start = ((s8[7340032]{0:T(1024)(128)(4,1)}), s8[3145728]{0:T(1024)(128)(4,1)S(1)}, s32[]{:S(2)}) async-start(s8[7340032]{0:T(1024)(128)(4,1)} %bitcast.190), calls=%async_computation.4 | async-start | bytes 6291456
  159.0 9.4 %slice-start.1 = ((s8[7340032]{0:T(1024)(128)(4,1)}), s8[4194304]{0:T(1024)(128)(4,1)S(1)}, s32[]{:S(2)}) async-start(s8[7340032]{0:T(1024)(128)(4,1)} %bitcast.190), calls=%async_computation.5 | async-start | bytes 8388608
  159.0 9.4 %copy-start.3 = (bf16[14,4,128,128]{3,2,1,0:T(8,128)(2,1)S(1)}, bf16[14,4,128,128]{3,2,1,0:T(8,128)(2,1)}, u32[]{:S(2)}) copy-start(bf16[14,4,128,128]{3,2,1,0:T(8,128)(2,1)} %param.17) | copy-start | bytes 5505028
  159.0 9.4 %copy-start.5 = (bf16[512,14,128,1]{2,0,3,1:T(8,128)(2,1)S(1)}, bf16[512,14,128,1]{2,0,3,1:T(8,128)(2,1)}, u32[]{:S(2)}) copy-start(bf16[512,14,128,1]{2,0,3,1:T(8,128)(2,1)} %copy-done.4) | copy-start | bytes 5505028
  159.0 12.8 %slice-start.4 = ((s8[7340032]{0:T(1024)(128)(4,1)}), s8[4194304]{0:T(1024)(128)(4,1)S(1)}, s32[]{:S(2)}) async-start(s8[7340032]{0:T(1024)(128)(4,1)} %bitcast.194), calls=%async_computation.8 | async-start | bytes 8388608
  168.4 3.4 slice-start.5
  185.8 239.9 %collective-permute-start.2 = (bf16[3,14,4,128,128]{4,3,2,1,0:T(8,128)(2,1)S(1)}, bf16[3,14,4,128,128]{4,3,2,1,0:T(8,128)(2,1)}, u32[]{:S(2)}, u32[]{:S(2)}) collective-permute-start(bf16[3,14,4,128,128]{4,3,2,1,0:T(8,128)(2,1)S(1)} %param.4), channel_id=1, source_target_pairs={{0,16},{4,20},{8,24},{12,28},{16,0},{20,4},{24,8},{28,12},{1,17},{... | collective-permute-start | bytes 16515080 | tf_op jit(solution)/shard_map/cond/branch_2_fun/ppermute | solution.py:22
Sparse Core Ops, SparseCore 0:
  10.1 25.5 all-gather.4
  37.8 22.8 all-gather.2
  154.4 44.5 reduce-scatter.1
where the time goes:
time: 447 us; the launch traced here: 441 us
  waiting for transfers between devices  257 us (57%)
  matrix products  81.4 us (18%)
  local copies, waits for them, and re-layouts  70 us (16%)
  between operations  15.1 us (3%)
  other arithmetic  15 us (3%)
    ppermute x1, waiting for transfers between devices, passed_along(): return lax.ppermute(value, axis, pairs)  237 us
    all_gather x1, waiting for transfers between devices, per_device(): lax.all_gather(tokens, 'tp', axis=0, tiled=True)  19.2 us
    dot_general x1, matrix products, per_device(): jnp.einsum('rjkc,jkb->rbc', up_back, up_onehot, precision=lax.Precision.H...  17.2 us
    dot_general x1, matrix products, per_device(): jnp.einsum('rjkc,jkb->rbc', gate_back, gate_onehot, precision=lax.Precisi...  16.8 us
    gather x2, local copies, waits for them, and re-layouts, per_device(): down_input = jnp.take(cotangent_blocks, down_columns, axis=1)  16.1 us
    gather x2, local copies, waits for them, and re-layouts, per_device(): up_input = jnp.take(token_blocks, up_rows, axis=1)  15.9 us
    gather x2, local copies, waits for them, and re-layouts, per_device(): gate_input = jnp.take(token_blocks, gate_rows, axis=1)  15.8 us
    unnamed x34, local copies, waits for them, and re-layouts  12.4 us
  transfers between devices with their start and end apart: 4, of which 2 were waited for; matrix products, arithmetic and copies ran while one was open for 18% of the time, Pallas kernels for 0%

commit v1 on v0

v1 whole, which is shorter than its diff:
```python
import functools

import jax
import jax.numpy as jnp
from jax import lax
from jax.experimental import pallas as pl
from jax.experimental.pallas import tpu as pltpu
from jax.sharding import PartitionSpec as P

LEARN_RATE = 0.5
PIECES = 4
FIRST = 2
LATER = 3
VMEM_LIMIT = 60 * 1024 * 1024
F32 = jnp.float32
BF16 = jnp.bfloat16


def gather_kernel(rows, tok, cot, all_tok, all_cot, own_sem, sib_send, sib_recv, far_send, far_recv, fwd_send, fwd_recv):
    me = lax.axis_index("tp")
    sibling = me + 1 - 2 * lax.rem(me, 2)
    far = lax.rem(me + 2, 4)
    barrier = pltpu.get_barrier_semaphore()
    for other in (sibling, far):
        pl.semaphore_signal(barrier, inc=1, device_id={"tp": other}, device_id_type=pl.DeviceIdType.MESH)
    pl.semaphore_wait(barrier, 2)
    pairs = ((tok, all_tok), (cot, all_cot))
    part = rows // PIECES
    far_copies = []
    for a, (own, gathered) in enumerate(pairs):
        for i in range(PIECES):
            span = pl.ds(i * part, part)
            copy = pltpu.make_async_remote_copy(
                src_ref=own.at[span],
                dst_ref=gathered.at[me, span],
                send_sem=far_send.at[a, i],
                recv_sem=far_recv.at[a, i],
                device_id={"tp": far},
                device_id_type=pl.DeviceIdType.MESH,
            )
            copy.start()
            far_copies.append(copy)
    near_copies = []
    own_copies = []
    for a, (own, gathered) in enumerate(pairs):
        copy = pltpu.make_async_remote_copy(
            src_ref=own,
            dst_ref=gathered.at[me],
            send_sem=sib_send.at[a],
            recv_sem=sib_recv.at[a],
            device_id={"tp": sibling},
            device_id_type=pl.DeviceIdType.MESH,
        )
        copy.start()
        near_copies.append(copy)
        mine = pltpu.make_async_copy(own, gathered.at[me], own_sem.at[a])
        mine.start()
        own_copies.append(mine)
    forwards = []
    for a, (own, gathered) in enumerate(pairs):
        for i in range(PIECES):
            far_copies[a * PIECES + i].wait_recv()
            span = pl.ds(i * part, part)
            copy = pltpu.make_async_remote_copy(
                src_ref=gathered.at[far, span],
                dst_ref=gathered.at[far, span],
                send_sem=fwd_send.at[a, i],
                recv_sem=fwd_recv.at[a, i],
                device_id={"tp": sibling},
                device_id_type=pl.DeviceIdType.MESH,
            )
            copy.start()
            forwards.append(copy)
    for copy in far_copies:
        copy.wait_send()
    for copy in near_copies + own_copies + forwards:
        copy.wait()


def gathered_rows(tokens, cotangent):
    rows, width = tokens.shape
    count = lax.axis_size("tp")
    assert count == 4
    shape = jax.ShapeDtypeStruct((count, rows, width), tokens.dtype)
    dma = pltpu.SemaphoreType.DMA
    both = pl.pallas_call(
        functools.partial(gather_kernel, rows),
        out_shape=(shape, shape),
        in_specs=[pl.BlockSpec(memory_space=pl.ANY)] * 2,
        out_specs=(pl.BlockSpec(memory_space=pl.ANY),) * 2,
        scratch_shapes=[
            dma((2,)),
            dma((2,)),
            dma((2,)),
            dma((2, PIECES)),
            dma((2, PIECES)),
            dma((2, PIECES)),
            dma((2, PIECES)),
        ],
        compiler_params=pltpu.CompilerParams(collective_id=0, has_side_effects=True),
    )(tokens, cotangent)
    return [part.reshape(count * rows, width) for part in both]


def dot(a, b, dims):
    return lax.dot_general(a, b, (dims, ((), ())), preferred_element_type=F32)


def step_kernel(offset, first, keep, edge, gate_rows, up_rows, down_columns, x, g, wg, wu, wd, *rest):
    fresh, total = rest[-2:]
    scale = (keep * edge) ** (-0.5)
    j = offset + pl.program_id(0)

    @pl.when(pl.program_id(0) == 0)
    def _():
        total[...] = jnp.zeros_like(total) if first else rest[0][...]

    def picked(source, rows):
        return jnp.concatenate(
            [source[:, pl.ds(pl.multiple_of(rows[j, k] * edge, edge), edge)] for k in range(keep)], axis=1
        )

    def flat(w):
        return w[0].reshape(keep * edge, edge)

    gate_in = picked(x, gate_rows)
    up_in = picked(x, up_rows)
    down_in = picked(g, down_columns)
    gate = scale * dot(gate_in, flat(wg), ((1,), (0,)))
    up = scale * dot(up_in, flat(wu), ((1,), (0,)))
    hidden_grad = jnp.zeros_like(gate)
    for k in range(keep):
        hidden_grad += dot(down_in[:, k * edge : (k + 1) * edge], wd[0, k], ((1,), (1,)))
    hidden_grad = scale * hidden_grad
    sig = jax.nn.sigmoid(gate)
    act = gate * sig
    hidden = (act * up).astype(BF16)
    gate_signal = (hidden_grad * up * sig * (1.0 + gate * (1.0 - sig))).astype(BF16)
    up_signal = (hidden_grad * act).astype(BF16)

    def step(w, grad):
        grad = (scale * grad).astype(BF16).astype(F32)
        return (w.astype(F32) - LEARN_RATE * grad).astype(BF16)

    def side(i, w, signal, inputs, turned):
        grad = dot(signal, inputs, ((0,), (0,)))
        for k in range(keep):
            part = grad[:, k * edge : (k + 1) * edge]
            fresh[i, 0, k] = step(w[0, k], part.T if turned else part)

    side(2, wd, hidden, down_in, False)
    side(0, wg, gate_signal, gate_in, True)
    side(1, wu, up_signal, up_in, True)
    for w, signal, rows in ((wg, gate_signal, gate_rows), (wu, up_signal, up_rows)):
        for k in range(keep):
            back = dot(signal, w[0, k], ((1,), (1,)))
            columns = pl.ds(pl.multiple_of(rows[j, k] * edge, edge), edge)
            total[:, columns] += back


def chunk_step(offset, size, total, rows, x, g, weights):
    keep, edge = weights[0].shape[1:3]
    whole = pl.BlockSpec(x.shape, lambda j, *_: (0, 0))
    block = pl.BlockSpec((1, keep, edge, edge), lambda j, *_: (offset + j, 0, 0, 0))
    first = total is None
    return pl.pallas_call(
        functools.partial(step_kernel, offset, first, keep, edge),
        grid_spec=pltpu.PrefetchScalarGridSpec(
            num_scalar_prefetch=3,
            grid=(size,),
            in_specs=[whole, whole, block, block, block] + ([] if first else [whole]),
            out_specs=[pl.BlockSpec((3, 1, keep, edge, edge), lambda j, *_: (0, j, 0, 0, 0)), whole],
        ),
        out_shape=[
            jax.ShapeDtypeStruct((3, size, keep, edge, edge), BF16),
            jax.ShapeDtypeStruct(x.shape, F32),
        ],
        compiler_params=pltpu.CompilerParams(vmem_limit_bytes=VMEM_LIMIT),
        cost_estimate=pl.CostEstimate(flops=1, bytes_accessed=1, transcendentals=0),
    )(*rows, x, g, *weights, *([] if first else [total]))


def mean_kernel(own, peer, *rest):
    for i, out in enumerate(rest[-3:]):
        out[0] = ((own[i, 0].astype(F32) + peer[i, 0].astype(F32)) * 0.5).astype(BF16)


def chunk_mean(offset, own, peer, outs, shape):
    _, size, keep, edge, _ = own.shape
    part = pl.BlockSpec((3, 1, keep, edge, edge), lambda j: (0, j, 0, 0, 0))
    out = pl.BlockSpec((1, keep, edge, edge), lambda j: (offset + j, 0, 0, 0))
    given = [] if outs is None else list(outs)
    return pl.pallas_call(
        mean_kernel,
        grid=(size,),
        in_specs=[part, part] + [pl.BlockSpec(memory_space=pl.ANY)] * len(given),
        out_specs=[out] * 3,
        out_shape=[jax.ShapeDtypeStruct(shape, BF16)] * 3,
        input_output_aliases={2 + i: i for i in range(len(given))},
        compiler_params=pltpu.CompilerParams(vmem_limit_bytes=VMEM_LIMIT),
        cost_estimate=pl.CostEstimate(flops=1, bytes_accessed=1, transcendentals=0),
    )(own, peer, *given)


def sum_kernel(scale, own, *rest):
    out = rest[-1]
    value = scale * own[...]
    for part in rest[:-1]:
        value = value + part[...].astype(F32)
    out[...] = value.astype(BF16)


def summed_rows(scale, total):
    count = lax.axis_size("tp")
    me = lax.axis_index("tp")
    rows = total.shape[0] // count
    parts = []
    for turn in range(1, count):
        part = lax.dynamic_slice_in_dim(total, (me ^ turn) * rows, rows)
        pairs = [(source, source ^ turn) for source in range(count)]
        parts.append(lax.ppermute((scale * part).astype(BF16), "tp", pairs))
    own = lax.dynamic_slice_in_dim(total, me * rows, rows)
    return pl.pallas_call(
        functools.partial(sum_kernel, scale),
        out_shape=jax.ShapeDtypeStruct(own.shape, BF16),
        compiler_params=pltpu.CompilerParams(vmem_limit_bytes=VMEM_LIMIT),
        cost_estimate=pl.CostEstimate(flops=1, bytes_accessed=1, transcendentals=0),
    )(own, *parts)


def spans(count):
    first = min(FIRST, count)
    cuts = [first + (count - first) * i // LATER for i in range(LATER + 1)]
    return [(0, first)] + [(a, b - a) for a, b in zip(cuts, cuts[1:]) if b > a]


def exchanged(operands, distance):
    x, g, weights, rows = operands
    count = lax.axis_size("rep")
    pairs = [(source, (source + distance) % count) for source in range(count)]
    total = None
    own, peer = [], []
    for offset, size in spans(weights[0].shape[0]):
        fresh, total = chunk_step(offset, size, total, rows, x, g, weights)
        own.append(fresh)
        peer.append(lax.ppermute(fresh, "rep", pairs))
    keep, edge = weights[0].shape[1:3]
    input_grad = summed_rows((keep * edge) ** (-0.5), total)
    outs = None
    for (offset, _), mine, theirs in zip(spans(weights[0].shape[0]), own, peer):
        outs = chunk_mean(offset, mine, theirs, outs, weights[0].shape)
    return (input_grad, *outs)


def per_device(tokens, cotangent, gate_blocks, up_blocks, down_blocks, gate_rows, up_rows, down_columns, step_index):
    x, g = gathered_rows(tokens, cotangent)
    levels = lax.axis_size("rep").bit_length() - 1
    branches = [functools.partial(exchanged, distance=2**exponent) for exponent in range(levels)]
    operands = (x, g, (gate_blocks, up_blocks, down_blocks), (gate_rows, up_rows, down_columns))
    return tuple(lax.switch(step_index[0] % levels, branches, operands))


def solution(mesh):
    blocks = P(("rep", "tp"), None, None, None)
    table = P("tp", None)
    rows = P(("rep", "tp"), None)
    return jax.shard_map(
        per_device,
        mesh=mesh,
        in_specs=(rows, rows, blocks, blocks, blocks, table, table, table, P()),
        out_specs=(rows, blocks, blocks, blocks),
        check_vma=False,
    )
```

time: 447 us -> 197 us (0.44); the launches traced: 441 us -> 196 us
  waiting for transfers between devices: 257 us -> 84.1 us
  Pallas kernels: 0 us -> 92.2 us
  matrix products: 81.4 us -> 0 us
  local copies, waits for them, and re-layouts: 70 us -> 7.85 us
  between operations: 15.1 us -> 1.3 us
  other arithmetic: 15 us -> 3.68 us
    ppermute x1 -> x7, waiting for transfers between devices: 237 us -> 84.1 us  [the longest x4 57.4 us: exchanged(): peer.append(lax.ppermute(fresh, 'rep', pairs))]
    pallas_call x0 -> x10, Pallas kernels: none -> 92.2 us  [the longest x4 47.6 us: chunk_step(): pl.pallas_call(functools.partial(step_kernel, offset, first, keep, edge),...]
    dot_general x10 -> x0, matrix products: 81.4 us -> none  [the longest x1 17.2 us: per_device(): jnp.einsum('rjkc,jkb->rbc', up_back, up_onehot, precision=lax.Precision.H...]
    gather x6 -> x0, local copies, waits for them, and re-layouts: 47.8 us -> none  [the longest x2 16.1 us: per_device(): down_input = jnp.take(cotangent_blocks, down_columns, axis=1)]
    all_gather x2 -> x0, waiting for transfers between devices: 19.2 us -> none  [the longest x1 19.2 us: per_device(): lax.all_gather(tokens, 'tp', axis=0, tiled=True)]
    unnamed x34 -> x2, local copies, waits for them, and re-layouts: 12.4 us -> 0.79 us
    reshape x2 -> x0, local copies, waits for them, and re-layouts: 6.06 us -> none  [the longest x1 3.03 us: per_device(): cotangent_blocks = all_cotangent.reshape(row_total, width_blocks, edge)]
    convert_element_type x2 -> x1, other arithmetic: 8.21 us -> 3.68 us  [summed_rows(): parts.append(lax.ppermute((scale * part).astype(BF16), 'tp', pairs))]
  transfers between devices with their start and end apart: 4 -> 7, of which waited for: 2 -> 4; matrix products, arithmetic and copies ran while one was open for 18% -> 2% of each run, Pallas kernels for 0% -> 19%
where the time goes in v1:
time: 197 us; the launch traced here: 196 us
  Pallas kernels  92.2 us (47%)
  waiting for transfers between devices  84.1 us (43%)
  local copies, waits for them, and re-layouts  7.85 us (4%)
  starting transfers between devices  6.59 us (3%)
  other arithmetic  3.68 us (2%)
    ppermute x4, waiting for transfers between devices, exchanged(): peer.append(lax.ppermute(fresh, 'rep', pairs))  57.4 us
    pallas_call x4, Pallas kernels, chunk_step(): pl.pallas_call(functools.partial(step_kernel, offset, first, keep, edge),...  47.6 us
    pallas_call x1, Pallas kernels, gathered_rows(): pl.pallas_call(functools.partial(gather_kernel, rows), out_shape=(shape,...  28.8 us
    ppermute x3, waiting for transfers between devices, summed_rows(): parts.append(lax.ppermute((scale * part).astype(BF16), 'tp', pairs))  26.7 us
    pallas_call x4, Pallas kernels, chunk_mean(): pl.pallas_call(mean_kernel, grid=(size,), in_specs=[part, part] + [pl.Blo...  13.8 us
    ppermute x4, starting transfers between devices, exchanged(): peer.append(lax.ppermute(fresh, 'rep', pairs))  4.97 us
    another operation x3, local copies, waits for them, and re-layouts  4.08 us
  transfers between devices with their start and end apart: 7, of which 4 were waited for; matrix products, arithmetic and copies ran while one was open for 2% of the time, Pallas kernels for 19%

profile of v1, /device:TPU:0, one launch (start us, length us, event | category | flops | bytes accessed | tf_op | source)
XLA Modules:
  0.0 195.9 jit_solution(8594052607379036642)
XLA Ops:
  1.3 28.8 %shard_map.123 = (bf16[4,128,2048]{2,1,0:T(8,128)(2,1)S(1)}, bf16[4,128,2048]{2,1,0:T(8,128)(2,1)}) custom-call(bf16[128,2048]{1,0:T(8,128)(2,1)} %tok.1, bf16[128,2048]{1,0:T(8,128)(2,1)} %cot.1), custom_call_target="tpu_custom_call" | custom-call | tf_op jit(solution)/shard_map/pallas_call | solution.py:86
  30.1 165.0 %conditional.1 = (bf16[14,4,128,128]{3,2,1,0:T(8,128)(2,1)}, bf16[14,4,128,128]{3,2,1,0:T(8,128)(2,1)}, bf16[14,4,128,128]{3,2,1,0:T(8,128)(2,1)}, bf16[128,2048]{1,0:T(8,128)(2,1)S(1)}) conditional(s32[]{:T(128)} %clamp.3, (s32[14,4]{0,1:T(4,128)}, s32[14,4]{0,1:T(4,128)}, s32[14,4]{0,1:T(4,128)}, bf16[512,2048]{1,0:T(8,128)(2,1)S(1)}, ...), branch_computations={%region_0.1_spmd, %region_1.2_spmd, %region_2.3_spmd} | conditional | flops 1572894 | bytes 61343800 | solution.py:260
  30.3 1.4 copy.46.gate_rows
  31.7 1.4 copy.47.up_rows
  33.1 1.4 copy.48.down_columns
  34.4 0.0 copy-start.1
  34.4 8.8 %branch_1_fun.9 = (bf16[3,2,4,128,128]{4,3,2,1,0:T(8,128)(2,1)}, f32[512,2048]{1,0:T(8,128)}) custom-call(s32[14,4]{1,0:T(8,128)} %copy.46.gate_rows, s32[14,4]{1,0:T(8,128)} %copy.47.up_rows, s32[14,4]{1,0:T(8,128)} %copy.48.down_columns, bf16[512,2048]{1,0:T(8,128)(2,1)S(1)} %get-tuple-element.79.x, bf16[512,2048]{1,0:T(8,128)(2,1)} %get-tuple-element.80.g, ...), custom_call_target="tpu_custom_call" | custom-call | flops 1 | bytes 1 | tf_op jit(solution)/shard_map/cond/branch_1_fun/pallas_call | solution.py:166
  43.2 0.0 copy-done.1
  43.2 13.0 %branch_1_fun.10 = (bf16[3,4,4,128,128]{4,3,2,1,0:T(8,128)(2,1)}, f32[512,2048]{1,0:T(8,128)}) custom-call(s32[14,4]{1,0:T(8,128)} %copy.46.gate_rows, s32[14,4]{1,0:T(8,128)} %copy.47.up_rows, s32[14,4]{1,0:T(8,128)} %copy.48.down_columns, bf16[512,2048]{1,0:T(8,128)(2,1)S(1)} %get-tuple-element.79.x, bf16[512,2048]{1,0:T(8,128)(2,1)} %get-tuple-element.80.g, ...), custom_call_target="tpu_custom_call" | custom-call | flops 1 | bytes 1 | tf_op jit(solution)/shard_map/cond/branch_1_fun/pallas_call | solution.py:166
  56.2 1.6 collective-permute-start.12
  57.7 13.0 %branch_1_fun.11 = (bf16[3,4,4,128,128]{4,3,2,1,0:T(8,128)(2,1)}, f32[512,2048]{1,0:T(8,128)}) custom-call(s32[14,4]{1,0:T(8,128)} %copy.46.gate_rows, s32[14,4]{1,0:T(8,128)} %copy.47.up_rows, s32[14,4]{1,0:T(8,128)} %copy.48.down_columns, bf16[512,2048]{1,0:T(8,128)(2,1)S(1)} %get-tuple-element.79.x, bf16[512,2048]{1,0:T(8,128)(2,1)} %get-tuple-element.80.g, ...), custom_call_target="tpu_custom_call" | custom-call | flops 1 | bytes 1 | tf_op jit(solution)/shard_map/cond/branch_1_fun/pallas_call | solution.py:166
  70.7 1.6 collective-permute-start.11
  72.3 12.9 %branch_1_fun.12 = (bf16[3,4,4,128,128]{4,3,2,1,0:T(8,128)(2,1)}, f32[512,2048]{1,0:T(8,128)}) custom-call(s32[14,4]{1,0:T(8,128)} %copy.46.gate_rows, s32[14,4]{1,0:T(8,128)} %copy.47.up_rows, s32[14,4]{1,0:T(8,128)} %copy.48.down_columns, bf16[512,2048]{1,0:T(8,128)(2,1)S(1)} %get-tuple-element.79.x, bf16[512,2048]{1,0:T(8,128)(2,1)} %get-tuple-element.80.g, ...), custom_call_target="tpu_custom_call" | custom-call | flops 1 | bytes 1 | tf_op jit(solution)/shard_map/cond/branch_1_fun/pallas_call | solution.py:166
  85.2 1.6 collective-permute-start.10
  86.8 0.0 copy-start.7
  86.8 3.7 %multiply_convert_fusion.3 = (bf16[128,2048]{1,0:T(8,128)(2,1)S(1)}, bf16[128,2048]{1,0:T(8,128)(2,1)S(1)}, bf16[128,2048]{1,0:T(8,128)(2,1)S(1)}, f32[128,2048]{1,0:T(8,128)}) fusion(f32[512,2048]{1,0:T(8,128)} %get-tuple-element.87, s32[]{:T(128)S(6)} %select_n.37, s32[]{:T(128)S(6)} %select_n.36, s32[]{:T(128)S(6)} %select_n.35, s32[]{:T(128)S(6)} %select_n.34), kind=kLoop, calls=%fused_computation.4 | loop fusion | flops 1572864 | bytes 6815760 | tf_op jit(solution)/shard_map/cond/branch_1_fun/convert_element_type | solution.py:221
  90.5 0.0 collective-permute-start.7
  90.5 1.1 collective-permute-start.8
  91.6 0.8 collective-permute-done.7.rest_0_
  92.4 0.0 copy-start.14
  92.4 0.0 copy-done.7
  92.4 0.2 collective-permute-start.13
  92.6 12.2 %collective-permute-done.8.rest_1_ = bf16[128,2048]{1,0:T(8,128)(2,1)S(1)} collective-permute-done((bf16[128,2048]{1,0:T(8,128)(2,1)S(1)}, bf16[128,2048]{1,0:T(8,128)(2,1)S(1)}, u32[]{:S(2)}, u32[]{:S(2)}) %collective-permute-start.8) | collective-permute-done | bytes 524320 | tf_op jit(solution)/shard_map/cond/branch_1_fun/ppermute | solution.py:221
  104.9 0.0 copy-start.17
  104.9 0.5 collective-permute-start.9
  105.4 13.7 %collective-permute-done.9.rest_2_ = bf16[128,2048]{1,0:T(8,128)(2,1)S(1)} collective-permute-done((bf16[128,2048]{1,0:T(8,128)(2,1)S(1)}, bf16[128,2048]{1,0:T(8,128)(2,1)S(1)}, u32[]{:S(2)}, u32[]{:S(2)}) %collective-permute-start.9) | collective-permute-done | bytes 524320 | tf_op jit(solution)/shard_map/cond/branch_1_fun/ppermute | solution.py:221
  119.1 0.0 copy-done.14
  119.1 0.0 copy-done.17
  119.1 0.0 copy-start.20
  119.1 0.8 copy-done.20
  119.9 1.9 branch_1_fun.13
  121.8 57.4 %collective-permute-done.13.peer = bf16[3,2,4,128,128]{4,3,2,1,0:T(8,128)(2,1)S(1)} collective-permute-done((bf16[3,2,4,128,128]{4,3,2,1,0:T(8,128)(2,1)S(1)}, bf16[3,2,4,128,128]{4,3,2,1,0:T(8,128)(2,1)S(1)}, u32[]{:S(2)}, u32[]{:S(2)}) %collective-permute-start.13) | collective-permute-done | bytes 786464 | tf_op jit(solution)/shard_map/cond/branch_1_fun/ppermute | solution.py:246
  179.2 0.0 copy-start.10
  179.2 0.9 copy-done.10
  180.1 2.1 %branch_1_fun.14 = (bf16[14,4,128,128]{3,2,1,0:T(8,128)(2,1)}, bf16[14,4,128,128]{3,2,1,0:T(8,128)(2,1)}, bf16[14,4,128,128]{3,2,1,0:T(8,128)(2,1)}) custom-call(bf16[3,2,4,128,128]{4,3,2,1,0:T(8,128)(2,1)} %get-tuple-element.91.own, bf16[3,2,4,128,128]{4,3,2,1,0:T(8,128)(2,1)} %copy-done.10), custom_call_target="tpu_custom_call" | custom-call | flops 1 | bytes 1 | tf_op jit(solution)/shard_map/cond/branch_1_fun/pallas_call | solution.py:193
  182.2 0.0 collective-permute-done.12.peer
  182.2 3.9 %branch_1_fun.15 = (bf16[14,4,128,128]{3,2,1,0:T(8,128)(2,1)}, bf16[14,4,128,128]{3,2,1,0:T(8,128)(2,1)}, bf16[14,4,128,128]{3,2,1,0:T(8,128)(2,1)}) custom-call(bf16[3,4,4,128,128]{4,3,2,1,0:T(8,128)(2,1)} %get-tuple-element.90.own, ...), custom_call_target="tpu_custom_call", output_to_operand_aliasing={{0}: (2, {}), {1}: (3, {}), {2}: (4, {})} | custom-call | flops 1 | bytes 1 | tf_op jit(solution)/shard_map/cond/branch_1_fun/pallas_call | solution.py:193
  186.1 0.0 collective-permute-done.11.peer
  186.1 3.9 %branch_1_fun.16 = (bf16[14,4,128,128]{3,2,1,0:T(8,128)(2,1)}, bf16[14,4,128,128]{3,2,1,0:T(8,128)(2,1)}, bf16[14,4,128,128]{3,2,1,0:T(8,128)(2,1)}) custom-call(bf16[3,4,4,128,128]{4,3,2,1,0:T(8,128)(2,1)} %get-tuple-element.89.own, ...), custom_call_target="tpu_custom_call", output_to_operand_aliasing={{0}: (2, {}), {1}: (3, {}), {2}: (4, {})} | custom-call | flops 1 | bytes 1 | tf_op jit(solution)/shard_map/cond/branch_1_fun/pallas_call | solution.py:193
  190.0 0.0 collective-permute-done.10.peer
  190.0 0.0 copy-start.4
  190.0 1.2 copy-done.4
  191.2 3.9 %branch_1_fun.17 = (bf16[14,4,128,128]{3,2,1,0:T(8,128)(2,1)}, bf16[14,4,128,128]{3,2,1,0:T(8,128)(2,1)}, bf16[14,4,128,128]{3,2,1,0:T(8,128)(2,1)}) custom-call(bf16[3,4,4,128,128]{4,3,2,1,0:T(8,128)(2,1)} %get-tuple-element.88.own, bf16[3,4,4,128,128]{4,3,2,1,0:T(8,128)(2,1)} %copy-done.4, ...), custom_call_target="tpu_custom_call", output_to_operand_aliasing={{0}: (2, {}), {1}: (3, {}), {2}: (4, {})} | custom-call | flops 1 | bytes 1 | tf_op jit(solution)/shard_map/cond/branch_1_fun/pallas_call | solution.py:193
  195.1 0.0 copy-start.12
  195.1 0.8 copy-done.12
Async XLA Ops:
  34.4 8.8 %copy-start.1 = (bf16[14,4,128,128]{3,2,1,0:T(8,128)(2,1)S(1)}, bf16[14,4,128,128]{3,2,1,0:T(8,128)(2,1)}, u32[]{:S(2)}) copy-start(bf16[14,4,128,128]{3,2,1,0:T(8,128)(2,1)} %get-tuple-element.81.wg) | copy-start | bytes 5505028 | tf_op jit(solution)/shard_map/cond
  56.2 126.1 %collective-permute-start.12 = (bf16[3,4,4,128,128]{4,3,2,1,0:T(8,128)(2,1)}, bf16[3,4,4,128,128]{4,3,2,1,0:T(8,128)(2,1)}, u32[]{:S(2)}, u32[]{:S(2)}) collective-permute-start(bf16[3,4,4,128,128]{4,3,2,1,0:T(8,128)(2,1)} %get-tuple-element.90.own), channel_id=1, source_target_pairs={{0,8},{4,12},{8,16},{12,20},{16,24},{20,28},{24,0},{28,4},{1,9},{5... | collective-permute-start | bytes 4718600 | tf_op jit(solution)/shard_map/cond/branch_1_fun/ppermute | solution.py:246
  70.7 115.4 %collective-permute-start.11 = (bf16[3,4,4,128,128]{4,3,2,1,0:T(8,128)(2,1)}, bf16[3,4,4,128,128]{4,3,2,1,0:T(8,128)(2,1)}, u32[]{:S(2)}, u32[]{:S(2)}) collective-permute-start(bf16[3,4,4,128,128]{4,3,2,1,0:T(8,128)(2,1)} %get-tuple-element.89.own), channel_id=1, source_target_pairs={{0,8},{4,12},{8,16},{12,20},{16,24},{20,28},{24,0},{28,4},{1,9},{5... | collective-permute-start | bytes 4718600 | tf_op jit(solution)/shard_map/cond/branch_1_fun/ppermute | solution.py:246
  85.2 104.8 %collective-permute-start.10 = (bf16[3,4,4,128,128]{4,3,2,1,0:T(8,128)(2,1)}, bf16[3,4,4,128,128]{4,3,2,1,0:T(8,128)(2,1)S(1)}, u32[]{:S(2)}, u32[]{:S(2)}) collective-permute-start(bf16[3,4,4,128,128]{4,3,2,1,0:T(8,128)(2,1)} %get-tuple-element.88.own), channel_id=1, source_target_pairs={{0,8},{4,12},{8,16},{12,20},{16,24},{20,28},{24,0},{28,4},{1,9},{5... | collective-permute-start | bytes 4718600 | tf_op jit(solution)/shard_map/cond/branch_1_fun/ppermute | solution.py:246
  86.8 5.6 %copy-start.7 = (bf16[3,2,4,128,128]{4,3,2,1,0:T(8,128)(2,1)S(1)}, bf16[3,2,4,128,128]{4,3,2,1,0:T(8,128)(2,1)}, u32[]{:S(2)}) copy-start(bf16[3,2,4,128,128]{4,3,2,1,0:T(8,128)(2,1)} %get-tuple-element.91.own) | copy-start | bytes 2359300 | tf_op jit(solution)/shard_map/cond
  90.5 1.9 collective-permute-start.7
  90.5 14.3 %collective-permute-start.8 = (bf16[128,2048]{1,0:T(8,128)(2,1)S(1)}, bf16[128,2048]{1,0:T(8,128)(2,1)S(1)}, u32[]{:S(2)}, u32[]{:S(2)}) collective-permute-start(bf16[128,2048]{1,0:T(8,128)(2,1)S(1)} %get-tuple-element.170), channel_id=1, source_target_pairs={{0,2},{1,3},{2,0},{3,1},{4,6},{5,7},{6,4},{7,5},{8,10},{9,11},{10,... | collective-permute-start | bytes 1572872 | tf_op jit(solution)/shard_map/cond/branch_1_fun/ppermute | solution.py:221
  92.4 26.6 %copy-start.14 = (bf16[128,2048]{1,0:T(8,128)(2,1)}, bf16[128,2048]{1,0:T(8,128)(2,1)S(1)}, u32[]{:S(2)}) copy-start(bf16[128,2048]{1,0:T(8,128)(2,1)S(1)} %collective-permute-done.7.rest_0_) | copy-start | bytes 1572868 | tf_op jit(solution)/shard_map/cond
  92.4 86.7 %collective-permute-start.13 = (bf16[3,2,4,128,128]{4,3,2,1,0:T(8,128)(2,1)S(1)}, bf16[3,2,4,128,128]{4,3,2,1,0:T(8,128)(2,1)S(1)}, u32[]{:S(2)}, u32[]{:S(2)}) collective-permute-start(bf16[3,2,4,128,128]{4,3,2,1,0:T(8,128)(2,1)S(1)} %copy-done.7), channel_id=1, source_target_pairs={{0,8},{4,12},{8,16},{12,20},{16,24},{20,28},{24,0},{28,4},{1,9},{5... | collective-permute-start | bytes 2359304 | tf_op jit(solution)/shard_map/cond/branch_1_fun/ppermute | solution.py:246
  104.9 14.2 %copy-start.17 = (bf16[128,2048]{1,0:T(8,128)(2,1)}, bf16[128,2048]{1,0:T(8,128)(2,1)S(1)}, u32[]{:S(2)}) copy-start(bf16[128,2048]{1,0:T(8,128)(2,1)S(1)} %collective-permute-done.8.rest_1_) | copy-start | bytes 1572868 | tf_op jit(solution)/shard_map/cond
  104.9 14.2 %collective-permute-start.9 = (bf16[128,2048]{1,0:T(8,128)(2,1)S(1)}, bf16[128,2048]{1,0:T(8,128)(2,1)S(1)}, u32[]{:S(2)}, u32[]{:S(2)}) collective-permute-start(bf16[128,2048]{1,0:T(8,128)(2,1)S(1)} %get-tuple-element.169), channel_id=1, source_target_pairs={{0,3},{1,2},{2,1},{3,0},{4,7},{5,6},{6,5},{7,4},{8,11},{9,10},{10,... | collective-permute-start | bytes 1572872 | tf_op jit(solution)/shard_map/cond/branch_1_fun/ppermute | solution.py:221
  119.1 0.8 copy-start.20
  179.2 0.9 copy-start.10
  190.0 1.2 copy-start.4
  195.1 0.8 copy-start.12

commit v2 on v1

--- a/solution.py
+++ b/solution.py
@@ -10,7 +10,7 @@
 LEARN_RATE = 0.5
 PIECES = 4
 FIRST = 2
-LATER = 3
+LATER = 4
 VMEM_LIMIT = 60 * 1024 * 1024
 F32 = jnp.float32
 BF16 = jnp.bfloat16
@@ -106,10 +106,12 @@
     return lax.dot_general(a, b, (dims, ((), ())), preferred_element_type=F32)
 
 
-def step_kernel(offset, first, keep, edge, gate_rows, up_rows, down_columns, x, g, wg, wu, wd, *rest):
+def step_kernel(offset, first, keep, edge, table, x, g, wg, wu, wd, *rest):
     fresh, total = rest[-2:]
     scale = (keep * edge) ** (-0.5)
     j = offset + pl.program_id(0)
+    count = table.shape[0] // (3 * keep)
+    gate_rows, up_rows, down_columns = ((i * count + j) * keep for i in range(3))
 
     @pl.when(pl.program_id(0) == 0)
     def _():
@@ -117,7 +119,7 @@
 
     def picked(source, rows):
         return jnp.concatenate(
-            [source[:, pl.ds(pl.multiple_of(rows[j, k] * edge, edge), edge)] for k in range(keep)], axis=1
+            [source[:, pl.ds(pl.multiple_of(table[rows + k] * edge, edge), edge)] for k in range(keep)], axis=1
         )
 
     def flat(w):
@@ -154,11 +156,11 @@
     for w, signal, rows in ((wg, gate_signal, gate_rows), (wu, up_signal, up_rows)):
         for k in range(keep):
             back = dot(signal, w[0, k], ((1,), (1,)))
-            columns = pl.ds(pl.multiple_of(rows[j, k] * edge, edge), edge)
+            columns = pl.ds(pl.multiple_of(table[rows + k] * edge, edge), edge)
             total[:, columns] += back
 
 
-def chunk_step(offset, size, total, rows, x, g, weights):
+def chunk_step(offset, size, total, table, x, g, weights, arrived):
     keep, edge = weights[0].shape[1:3]
     whole = pl.BlockSpec(x.shape, lambda j, *_: (0, 0))
     block = pl.BlockSpec((1, keep, edge, edge), lambda j, *_: (offset + j, 0, 0, 0))
@@ -166,9 +168,10 @@
     return pl.pallas_call(
         functools.partial(step_kernel, offset, first, keep, edge),
         grid_spec=pltpu.PrefetchScalarGridSpec(
-            num_scalar_prefetch=3,
+            num_scalar_prefetch=1,
             grid=(size,),
-            in_specs=[whole, whole, block, block, block] + ([] if first else [whole]),
+            in_specs=[whole, whole, block, block, block] + ([] if first else [whole])
+            + [pl.BlockSpec(memory_space=pl.ANY)] * len(arrived),
             out_specs=[pl.BlockSpec((3, 1, keep, edge, edge), lambda j, *_: (0, j, 0, 0, 0)), whole],
         ),
         out_shape=[
@@ -177,7 +180,7 @@
         ],
         compiler_params=pltpu.CompilerParams(vmem_limit_bytes=VMEM_LIMIT),
         cost_estimate=pl.CostEstimate(flops=1, bytes_accessed=1, transcendentals=0),
-    )(*rows, x, g, *weights, *([] if first else [total]))
+    )(table, x, g, *weights, *([] if first else [total]), *arrived)
 
 
 def mean_kernel(own, peer, *rest):
@@ -235,13 +238,13 @@
 
 
 def exchanged(operands, distance):
-    x, g, weights, rows = operands
+    x, g, weights, table = operands
     count = lax.axis_size("rep")
     pairs = [(source, (source + distance) % count) for source in range(count)]
     total = None
     own, peer = [], []
     for offset, size in spans(weights[0].shape[0]):
-        fresh, total = chunk_step(offset, size, total, rows, x, g, weights)
+        fresh, total = chunk_step(offset, size, total, table, x, g, weights, peer[-2:-1])
         own.append(fresh)
         peer.append(lax.ppermute(fresh, "rep", pairs))
     keep, edge = weights[0].shape[1:3]
@@ -253,10 +256,11 @@
 
 
 def per_device(tokens, cotangent, gate_blocks, up_blocks, down_blocks, gate_rows, up_rows, down_columns, step_index):
+    table = jnp.concatenate([gate_rows, up_rows, down_columns]).reshape(-1)
     x, g = gathered_rows(tokens, cotangent)
     levels = lax.axis_size("rep").bit_length() - 1
     branches = [functools.partial(exchanged, distance=2**exponent) for exponent in range(levels)]
-    operands = (x, g, (gate_blocks, up_blocks, down_blocks), (gate_rows, up_rows, down_columns))
+    operands = (x, g, (gate_blocks, up_blocks, down_blocks), table)
     return tuple(lax.switch(step_index[0] % levels, branches, operands))
 
 

time: 197 us -> 169 us (0.86)
  waiting for transfers between devices: 84.1 us -> 53.3 us
  Pallas kernels: 92.2 us -> 99.1 us
  local copies, waits for them, and re-layouts: 7.85 us -> 4.72 us
    ppermute x3, waiting for transfers between devices: 26.7 us -> 10 us  [summed_rows(): parts.append(lax.ppermute((scale * part).astype(BF16), 'tp', pairs))]
    ppermute x4 -> x5, waiting for transfers between devices: 57.4 us -> 43.3 us  [exchanged(): peer.append(lax.ppermute(fresh, 'rep', pairs))]
    pallas_call x4 -> x5, Pallas kernels: 47.6 us -> 52.6 us  [chunk_step(): pl.pallas_call(functools.partial(step_kernel, offset, first, keep, edge),...]
    another operation x3 -> x1, local copies, waits for them, and re-layouts: 4.08 us -> 0.1 us
    pallas_call x4 -> x5, Pallas kernels: 13.8 us -> 15.7 us  [chunk_mean(): pl.pallas_call(mean_kernel, grid=(size,), in_specs=[part, part] + [pl.Blo...]
    ppermute x4 -> x5, starting transfers between devices: 4.97 us -> 3.16 us  [exchanged(): peer.append(lax.ppermute(fresh, 'rep', pairs))]
  transfers between devices with their start and end apart: 7 -> 8, of which waited for: 4 -> 5; matrix products, arithmetic and copies ran while one was open for 2% -> 2% of each run, Pallas kernels for 19% -> 35%
where the time goes in v2:
time: 169 us; the launch traced here: 168 us
  Pallas kernels  99.1 us (59%)
  waiting for transfers between devices  53.3 us (32%)
  starting transfers between devices  5.02 us (3%)
  local copies, waits for them, and re-layouts  4.72 us (3%)
  other arithmetic  4.6 us (3%)
    pallas_call x5, Pallas kernels, chunk_step(): pl.pallas_call(functools.partial(step_kernel, offset, first, keep, edge),...  52.6 us
    ppermute x5, waiting for transfers between devices, exchanged(): peer.append(lax.ppermute(fresh, 'rep', pairs))  43.3 us
    pallas_call x1, Pallas kernels, gathered_rows(): pl.pallas_call(functools.partial(gather_kernel, rows), out_shape=(shape,...  28.8 us
    pallas_call x5, Pallas kernels, chunk_mean(): pl.pallas_call(mean_kernel, grid=(size,), in_specs=[part, part] + [pl.Blo...  15.7 us
    ppermute x3, waiting for transfers between devices, summed_rows(): parts.append(lax.ppermute((scale * part).astype(BF16), 'tp', pairs))  10 us
    convert_element_type x1, other arithmetic, summed_rows(): parts.append(lax.ppermute((scale * part).astype(BF16), 'tp', pairs))  3.81 us
  transfers between devices with their start and end apart: 8, of which 5 were waited for; matrix products, arithmetic and copies ran while one was open for 2% of the time, Pallas kernels for 35%

profile of v2, /device:TPU:0, one launch (start us, length us, event | category | flops | bytes accessed | tf_op | source)
XLA Modules:
  0.0 168.3 jit_solution(9048203132537373241)
XLA Ops:
  1.3 28.8 %shard_map.132 = (bf16[4,128,2048]{2,1,0:T(8,128)(2,1)S(1)}, bf16[4,128,2048]{2,1,0:T(8,128)(2,1)}) custom-call(bf16[128,2048]{1,0:T(8,128)(2,1)} %tok.1, bf16[128,2048]{1,0:T(8,128)(2,1)} %cot.1), custom_call_target="tpu_custom_call" | custom-call | tf_op jit(solution)/shard_map/pallas_call | solution.py:86
  30.1 0.8 pad_add_fusion
  30.9 136.6 %conditional.1 = (bf16[14,4,128,128]{3,2,1,0:T(8,128)(2,1)}, bf16[14,4,128,128]{3,2,1,0:T(8,128)(2,1)}, bf16[14,4,128,128]{3,2,1,0:T(8,128)(2,1)}, bf16[128,2048]{1,0:T(8,128)(2,1)S(1)}) conditional(s32[]{:T(128)} %clamp.3, (s32[42,4]{0,1:T(4,128)S(1)}, bf16[4,128,2048]{2,1,0:T(8,128)(2,1)S(1)}, bf16[4,128,2048]{2,1,0:T(8,128)(2,1)}, ...), branch_computations={%region_0.1_spmd, %region_1.2_spmd, %region_2.3_spmd} | conditional | flops 1572896 | bytes 49286448 | solution.py:264
  31.0 0.1 copy.65
  31.2 0.7 reshape.23.table
  31.8 8.2 %branch_1_fun.11 = (bf16[3,2,4,128,128]{4,3,2,1,0:T(8,128)(2,1)}, f32[512,2048]{1,0:T(8,128)}) custom-call(s32[168]{0:T(256)} %reshape.23.table, bf16[512,2048]{1,0:T(8,128)(2,1)S(1)} %bitcast.12, bf16[512,2048]{1,0:T(8,128)(2,1)} %bitcast.27, bf16[14,4,128,128]{3,2,1,0:T(8,128)(2,1)} %get-tuple-element.157.wg, ...), custom_call_target="tpu_custom_call" | custom-call | flops 1 | bytes 1 | tf_op jit(solution)/shard_map/cond/branch_1_fun/pallas_call | solution.py:168
  40.1 1.6 collective-permute-start.8
  41.6 11.1 %branch_1_fun.12 = (bf16[3,3,4,128,128]{4,3,2,1,0:T(8,128)(2,1)}, f32[512,2048]{1,0:T(8,128)}) custom-call(s32[168]{0:T(256)} %reshape.23.table, bf16[512,2048]{1,0:T(8,128)(2,1)S(1)} %bitcast.13, bf16[512,2048]{1,0:T(8,128)(2,1)} %bitcast.28, bf16[14,4,128,128]{3,2,1,0:T(8,128)(2,1)} %get-tuple-element.157.wg, ...), custom_call_target="tpu_custom_call" | custom-call | flops 1 | bytes 1 | tf_op jit(solution)/shard_map/cond/branch_1_fun/pallas_call | solution.py:168
  52.7 1.6 collective-permute-start.9
  54.3 8.2 %collective-permute-done.8.rest_1_.peer = bf16[3,2,4,128,128]{4,3,2,1,0:T(8,128)(2,1)} collective-permute-done((bf16[3,2,4,128,128]{4,3,2,1,0:T(8,128)(2,1)}, bf16[3,2,4,128,128]{4,3,2,1,0:T(8,128)(2,1)}, u32[]{:S(2)}, u32[]{:S(2)}) %collective-permute-start.8) | collective-permute-done | bytes 786464 | tf_op jit(solution)/shard_map/cond/branch_1_fun/ppermute | solution.py:249
  62.5 11.1 %branch_1_fun.13 = (bf16[3,3,4,128,128]{4,3,2,1,0:T(8,128)(2,1)}, f32[512,2048]{1,0:T(8,128)}) custom-call(s32[168]{0:T(256)} %reshape.23.table, bf16[512,2048]{1,0:T(8,128)(2,1)S(1)} %bitcast.14, bf16[512,2048]{1,0:T(8,128)(2,1)} %bitcast.29, bf16[14,4,128,128]{3,2,1,0:T(8,128)(2,1)} %get-tuple-element.157.wg, ...), custom_call_target="tpu_custom_call" | custom-call | flops 1 | bytes 1 | tf_op jit(solution)/shard_map/cond/branch_1_fun/pallas_call | solution.py:168
  73.6 0.0 collective-permute-start.10
  73.6 14.1 %collective-permute-done.9.rest_1_.peer = bf16[3,3,4,128,128]{4,3,2,1,0:T(8,128)(2,1)S(1)} collective-permute-done((bf16[3,3,4,128,128]{4,3,2,1,0:T(8,128)(2,1)}, bf16[3,3,4,128,128]{4,3,2,1,0:T(8,128)(2,1)S(1)}, u32[]{:S(2)}, u32[]{:S(2)}) %collective-permute-start.9) | collective-permute-done | bytes 1179680 | tf_op jit(solution)/shard_map/cond/branch_1_fun/ppermute | solution.py:249
  87.7 0.0 copy-start.1
  87.7 1.0 copy-done.1
  88.7 11.1 %branch_1_fun.14 = (bf16[3,3,4,128,128]{4,3,2,1,0:T(8,128)(2,1)}, f32[512,2048]{1,0:T(8,128)}) custom-call(s32[168]{0:T(256)} %reshape.23.table, bf16[512,2048]{1,0:T(8,128)(2,1)S(1)} %bitcast.15, bf16[512,2048]{1,0:T(8,128)(2,1)} %bitcast.30, bf16[14,4,128,128]{3,2,1,0:T(8,128)(2,1)} %get-tuple-element.157.wg, ...), custom_call_target="tpu_custom_call" | custom-call | flops 1 | bytes 1 | tf_op jit(solution)/shard_map/cond/branch_1_fun/pallas_call | solution.py:168
  99.8 0.0 collective-permute-start.15
  99.8 13.2 %collective-permute-done.10.rest_1_.peer = bf16[3,3,4,128,128]{4,3,2,1,0:T(8,128)(2,1)} collective-permute-done((bf16[3,3,4,128,128]{4,3,2,1,0:T(8,128)(2,1)}, bf16[3,3,4,128,128]{4,3,2,1,0:T(8,128)(2,1)}, u32[]{:S(2)}, u32[]{:S(2)}) %collective-permute-start.10) | collective-permute-done | bytes 1179680 | tf_op jit(solution)/shard_map/cond/branch_1_fun/ppermute | solution.py:249
  113.1 11.1 %branch_1_fun.15 = (bf16[3,3,4,128,128]{4,3,2,1,0:T(8,128)(2,1)}, f32[512,2048]{1,0:T(8,128)}) custom-call(s32[168]{0:T(256)} %reshape.23.table, bf16[512,2048]{1,0:T(8,128)(2,1)S(1)} %bitcast.16, bf16[512,2048]{1,0:T(8,128)(2,1)} %bitcast.31, bf16[14,4,128,128]{3,2,1,0:T(8,128)(2,1)} %get-tuple-element.157.wg, ...), custom_call_target="tpu_custom_call" | custom-call | flops 1 | bytes 1 | tf_op jit(solution)/shard_map/cond/branch_1_fun/pallas_call | solution.py:168
  124.2 0.0 collective-permute-start.14
  124.2 3.8 %multiply_convert_fusion.3 = (bf16[128,2048]{1,0:T(8,128)(2,1)S(1)}, bf16[128,2048]{1,0:T(8,128)(2,1)S(1)}, bf16[128,2048]{1,0:T(8,128)(2,1)}, f32[128,2048]{1,0:T(8,128)}) fusion(f32[512,2048]{1,0:T(8,128)} %get-tuple-element.80, s32[]{:T(128)S(6)} %select_n.37, s32[]{:T(128)S(6)} %select_n.36, s32[]{:T(128)S(6)} %select_n.35, s32[]{:T(128)S(6)} %select_n.34), kind=kLoop, calls=%fused_computation.4 | loop fusion | flops 1572864 | bytes 6815760 | tf_op jit(solution)/shard_map/cond/branch_1_fun/convert_element_type | solution.py:224
  128.0 0.0 collective-permute-start.11
  128.0 1.1 collective-permute-start.12
  129.1 0.8 collective-permute-start.13
  129.9 2.1 %branch_1_fun.17 = (bf16[14,4,128,128]{3,2,1,0:T(8,128)(2,1)}, bf16[14,4,128,128]{3,2,1,0:T(8,128)(2,1)}, bf16[14,4,128,128]{3,2,1,0:T(8,128)(2,1)}) custom-call(bf16[3,2,4,128,128]{4,3,2,1,0:T(8,128)(2,1)} %get-tuple-element.75.own, bf16[3,2,4,128,128]{4,3,2,1,0:T(8,128)(2,1)} %collective-permute-done.8.rest_1_.peer), custom_call_target="tpu_custom_call" | custom-call | flops 1 | bytes 1 | tf_op jit(solution)/shard_map/cond/branch_1_fun/pallas_call | solution.py:196
  132.0 3.4 %branch_1_fun.18 = (bf16[14,4,128,128]{3,2,1,0:T(8,128)(2,1)}, bf16[14,4,128,128]{3,2,1,0:T(8,128)(2,1)}, bf16[14,4,128,128]{3,2,1,0:T(8,128)(2,1)}) custom-call(bf16[3,3,4,128,128]{4,3,2,1,0:T(8,128)(2,1)} %get-tuple-element.77.own, bf16[3,3,4,128,128]{4,3,2,1,0:T(8,128)(2,1)} %copy-done.1, ...), custom_call_target="tpu_custom_call", output_to_operand_aliasing={{0}: (2, {}), {1}: (3, {}), {2}: (4, {})} | custom-call | flops 1 | bytes 1 | tf_op jit(solution)/shard_map/cond/branch_1_fun/pallas_call | solution.py:196
  135.4 3.4 %branch_1_fun.19 = (bf16[14,4,128,128]{3,2,1,0:T(8,128)(2,1)}, bf16[14,4,128,128]{3,2,1,0:T(8,128)(2,1)}, bf16[14,4,128,128]{3,2,1,0:T(8,128)(2,1)}) custom-call(bf16[3,3,4,128,128]{4,3,2,1,0:T(8,128)(2,1)} %get-tuple-element.79.own, ...), custom_call_target="tpu_custom_call", output_to_operand_aliasing={{0}: (2, {}), {1}: (3, {}), {2}: (4, {})} | custom-call | flops 1 | bytes 1 | tf_op jit(solution)/shard_map/cond/branch_1_fun/pallas_call | solution.py:196
  138.8 0.0 collective-permute-done.15.peer
  138.8 0.0 copy-start.7
  138.8 1.1 copy-done.7
  139.9 3.4 %branch_1_fun.20 = (bf16[14,4,128,128]{3,2,1,0:T(8,128)(2,1)}, bf16[14,4,128,128]{3,2,1,0:T(8,128)(2,1)}, bf16[14,4,128,128]{3,2,1,0:T(8,128)(2,1)}) custom-call(bf16[3,3,4,128,128]{4,3,2,1,0:T(8,128)(2,1)} %get-tuple-element.82.own, bf16[3,3,4,128,128]{4,3,2,1,0:T(8,128)(2,1)} %copy-done.7, ...), custom_call_target="tpu_custom_call", output_to_operand_aliasing={{0}: (2, {}), {1}: (3, {}), {2}: (4, {})} | custom-call | flops 1 | bytes 1 | tf_op jit(solution)/shard_map/cond/branch_1_fun/pallas_call | solution.py:196
  143.3 0.0 collective-permute-done.11.rest_0_
  143.3 0.0 collective-permute-done.12.rest_1_
  143.3 10.0 %collective-permute-done.13.rest_2_ = bf16[128,2048]{1,0:T(8,128)(2,1)} collective-permute-done((bf16[128,2048]{1,0:T(8,128)(2,1)S(1)}, bf16[128,2048]{1,0:T(8,128)(2,1)}, u32[]{:S(2)}, u32[]{:S(2)}) %collective-permute-start.13) | collective-permute-done | bytes 524320 | tf_op jit(solution)/shard_map/cond/branch_1_fun/ppermute | solution.py:224
  153.3 1.9 %branch_1_fun.16 = bf16[128,2048]{1,0:T(8,128)(2,1)S(1)} custom-call(f32[128,2048]{1,0:T(8,128)} %get-tuple-element.190.own, bf16[128,2048]{1,0:T(8,128)(2,1)} %collective-permute-done.11.rest_0_, bf16[128,2048]{1,0:T(8,128)(2,1)} %collective-permute-done.12.rest_1_, bf16[128,2048]{1,0:T(8,128)(2,1)} %collective-permute-done.13.rest_2_), custom_call_target="tpu_custom_call" | custom-call | flops 1 | bytes 1 | tf_op jit(solution)/shard_map/cond/branch_1_fun/pallas_call | solution.py:226
  155.2 7.8 %collective-permute-done.14.peer = bf16[3,3,4,128,128]{4,3,2,1,0:T(8,128)(2,1)S(1)} collective-permute-done((bf16[3,3,4,128,128]{4,3,2,1,0:T(8,128)(2,1)}, bf16[3,3,4,128,128]{4,3,2,1,0:T(8,128)(2,1)S(1)}, u32[]{:S(2)}, u32[]{:S(2)}) %collective-permute-start.14) | collective-permute-done | bytes 1179680 | tf_op jit(solution)/shard_map/cond/branch_1_fun/ppermute | solution.py:249
  163.1 0.0 copy-start.4
  163.1 1.0 copy-done.4
  164.1 3.4 %branch_1_fun.21 = (bf16[14,4,128,128]{3,2,1,0:T(8,128)(2,1)}, bf16[14,4,128,128]{3,2,1,0:T(8,128)(2,1)}, bf16[14,4,128,128]{3,2,1,0:T(8,128)(2,1)}) custom-call(bf16[3,3,4,128,128]{4,3,2,1,0:T(8,128)(2,1)} %get-tuple-element.81.own, bf16[3,3,4,128,128]{4,3,2,1,0:T(8,128)(2,1)} %copy-done.4, ...), custom_call_target="tpu_custom_call", output_to_operand_aliasing={{0}: (2, {}), {1}: (3, {}), {2}: (4, {})} | custom-call | flops 1 | bytes 1 | tf_op jit(solution)/shard_map/cond/branch_1_fun/pallas_call | solution.py:196
  167.5 0.0 copy-start.9
  167.5 0.8 copy-done.9
Async XLA Ops:
  40.1 22.5 %collective-permute-start.8 = (bf16[3,2,4,128,128]{4,3,2,1,0:T(8,128)(2,1)}, bf16[3,2,4,128,128]{4,3,2,1,0:T(8,128)(2,1)}, u32[]{:S(2)}, u32[]{:S(2)}) collective-permute-start(bf16[3,2,4,128,128]{4,3,2,1,0:T(8,128)(2,1)} %get-tuple-element.75.own), channel_id=1, source_target_pairs={{0,8},{4,12},{8,16},{12,20},{16,24},{20,28},{24,0},{28,4},{1,9},{5... | collective-permute-start | bytes 2359304 | tf_op jit(solution)/shard_map/cond/branch_1_fun/ppermute | solution.py:249
  52.7 35.0 %collective-permute-start.9 = (bf16[3,3,4,128,128]{4,3,2,1,0:T(8,128)(2,1)}, bf16[3,3,4,128,128]{4,3,2,1,0:T(8,128)(2,1)S(1)}, u32[]{:S(2)}, u32[]{:S(2)}) collective-permute-start(bf16[3,3,4,128,128]{4,3,2,1,0:T(8,128)(2,1)} %get-tuple-element.77.own), channel_id=1, source_target_pairs={{0,8},{4,12},{8,16},{12,20},{16,24},{20,28},{24,0},{28,4},{1,9},{5... | collective-permute-start | bytes 3538952 | tf_op jit(solution)/shard_map/cond/branch_1_fun/ppermute | solution.py:249
  73.6 39.4 %collective-permute-start.10 = (bf16[3,3,4,128,128]{4,3,2,1,0:T(8,128)(2,1)}, bf16[3,3,4,128,128]{4,3,2,1,0:T(8,128)(2,1)}, u32[]{:S(2)}, u32[]{:S(2)}) collective-permute-start(bf16[3,3,4,128,128]{4,3,2,1,0:T(8,128)(2,1)} %get-tuple-element.79.own), channel_id=1, source_target_pairs={{0,8},{4,12},{8,16},{12,20},{16,24},{20,28},{24,0},{28,4},{1,9},{5... | collective-permute-start | bytes 3538952 | tf_op jit(solution)/shard_map/cond/branch_1_fun/ppermute | solution.py:249
  87.7 1.0 copy-start.1
  99.8 39.0 %collective-permute-start.15 = (bf16[3,3,4,128,128]{4,3,2,1,0:T(8,128)(2,1)}, bf16[3,3,4,128,128]{4,3,2,1,0:T(8,128)(2,1)S(1)}, u32[]{:S(2)}, u32[]{:S(2)}) collective-permute-start(bf16[3,3,4,128,128]{4,3,2,1,0:T(8,128)(2,1)} %get-tuple-element.82.own), channel_id=1, source_target_pairs={{0,8},{4,12},{8,16},{12,20},{16,24},{20,28},{24,0},{28,4},{1,9},{5... | collective-permute-start | bytes 3538952 | tf_op jit(solution)/shard_map/cond/branch_1_fun/ppermute | solution.py:249
  124.2 38.9 %collective-permute-start.14 = (bf16[3,3,4,128,128]{4,3,2,1,0:T(8,128)(2,1)}, bf16[3,3,4,128,128]{4,3,2,1,0:T(8,128)(2,1)S(1)}, u32[]{:S(2)}, u32[]{:S(2)}) collective-permute-start(bf16[3,3,4,128,128]{4,3,2,1,0:T(8,128)(2,1)} %get-tuple-element.81.own), channel_id=1, source_target_pairs={{0,8},{4,12},{8,16},{12,20},{16,24},{20,28},{24,0},{28,4},{1,9},{5... | collective-permute-start | bytes 3538952 | tf_op jit(solution)/shard_map/cond/branch_1_fun/ppermute | solution.py:249
  128.0 15.3 %collective-permute-start.11 = (bf16[128,2048]{1,0:T(8,128)(2,1)}, bf16[128,2048]{1,0:T(8,128)(2,1)}, u32[]{:S(2)}, u32[]{:S(2)}) collective-permute-start(bf16[128,2048]{1,0:T(8,128)(2,1)} %get-tuple-element.189), channel_id=1, source_target_pairs={{0,1},{1,0},{2,3},{3,2},{4,5},{5,4},{6,7},{7,6},{8,9},{9,8},{10,11... | collective-permute-start | bytes 1572872 | tf_op jit(solution)/shard_map/cond/branch_1_fun/ppermute | solution.py:224
  128.0 15.3 %collective-permute-start.12 = (bf16[128,2048]{1,0:T(8,128)(2,1)S(1)}, bf16[128,2048]{1,0:T(8,128)(2,1)}, u32[]{:S(2)}, u32[]{:S(2)}) collective-permute-start(bf16[128,2048]{1,0:T(8,128)(2,1)S(1)} %get-tuple-element.188), channel_id=1, source_target_pairs={{0,2},{1,3},{2,0},{3,1},{4,6},{5,7},{6,4},{7,5},{8,10},{9,11},{10,... | collective-permute-start | bytes 1572872 | tf_op jit(solution)/shard_map/cond/branch_1_fun/ppermute | solution.py:224
  129.1 24.2 %collective-permute-start.13 = (bf16[128,2048]{1,0:T(8,128)(2,1)S(1)}, bf16[128,2048]{1,0:T(8,128)(2,1)}, u32[]{:S(2)}, u32[]{:S(2)}) collective-permute-start(bf16[128,2048]{1,0:T(8,128)(2,1)S(1)} %get-tuple-element.187), channel_id=1, source_target_pairs={{0,3},{1,2},{2,1},{3,0},{4,7},{5,6},{6,5},{7,4},{8,11},{9,10},{10,... | collective-permute-start | bytes 1572872 | tf_op jit(solution)/shard_map/cond/branch_1_fun/ppermute | solution.py:224
  138.8 1.1 copy-start.7
  163.1 1.1 copy-start.4
  167.5 0.8 copy-start.9
